TPU v7x, 32 devices: a whole 2x2x4 slice. The times are simulated.
32 devices in a mesh: chan: 4 (over y, x), win: 8 (over z, core).
Axes of the slice: x: 2, y: 2, z: 4, core: 2. Of those that a mesh axis runs over, the one named last changes fastest.
Arguments:
- raw: bfloat16 [32, 3200, 1024], P('win', None, 'chan'), may hold values from -6 to 6
- offsets: int32 [32], P('win'), may hold values from 0 to 128
- quality: int32 [32, 1024], P('win', 'chan'), may hold values 0 or 1
Outputs:
- stack: bfloat16 [384, 2, 1024, 1024], P('win', None, 'chan')
All inputs are finite; a program needn't handle non-finite values. No bound on the sum of `quality` on one device may be relied on, other than what follows from the above.
Results may differ from a plain program's by a relative error of at most 0.0064.
Values may be sent and summed in bfloat16 or wider, within the bound.
No kernel may reach another device: no remote copies, remote signals or barrier semaphores. Data moves between devices by JAX's collectives and lax.ppermute only.
A program may use at most 256 MiB of HBM per device.

v0:
```python
import math

import jax
import jax.numpy as jnp
from jax import lax
from jax.sharding import PartitionSpec as P

F = 384
L = 3072
FIRST_BIN = 60


epsilon = 1e-05


def dft_table():
    sample_idx = jnp.arange(L, dtype=jnp.int32)
    bin_idx = FIRST_BIN + jnp.arange(F, dtype=jnp.int32)
    residue = bin_idx[:, None] * sample_idx[None, :] % L
    angles = residue.astype(jnp.float32) * (2.0 * math.pi / L)
    return jnp.concatenate([jnp.cos(angles), -jnp.sin(angles)], 0).astype(jnp.bfloat16)


def cross_spectra(mine, partner):
    stack_scale = 1.0 / math.sqrt(mine.shape[0])
    real_mine = mine[:, 0]
    imag_mine = mine[:, 1]
    real_other = partner[:, 0]
    imag_other = partner[:, 1]
    real_part = jnp.einsum(
        "wfi,wfj->fij", real_mine, real_other, preferred_element_type=jnp.float32
    )
    real_part = real_part + jnp.einsum(
        "wfi,wfj->fij", imag_mine, imag_other, preferred_element_type=jnp.float32
    )
    imag_part = jnp.einsum(
        "wfi,wfj->fij", imag_mine, real_other, preferred_element_type=jnp.float32
    )
    imag_part = imag_part - jnp.einsum(
        "wfi,wfj->fij", real_mine, imag_other, preferred_element_type=jnp.float32
    )
    return (jnp.stack([real_part, imag_part], 1) * stack_scale).astype(jnp.bfloat16)


def local(raw, offsets, quality):
    table = dft_table()

    def cut_window(segment, shift_at):
        return lax.dynamic_slice_in_dim(segment, shift_at, L, 0)

    windows = jax.vmap(cut_window)(raw, offsets)
    transform = jnp.einsum("kl,wlc->wkc", table, windows, preferred_element_type=jnp.float32)
    band_power = jnp.sum(transform * transform, axis=1, keepdims=True) / F
    whiten = lax.rsqrt(band_power + epsilon) * quality.astype(jnp.float32)[:, None, :]
    block_width = raw.shape[2]
    spectra = (transform * whiten).astype(jnp.bfloat16).reshape(raw.shape[0], 2, F, block_width)
    bin_local = lax.all_to_all(spectra, "win", split_axis=2, concat_axis=0, tiled=True)
    return cross_spectra(bin_local, lax.all_gather(bin_local, "chan", axis=3, tiled=True))


def solution(mesh):
    in_specs = (P("win", None, "chan"), P("win"), P("win", "chan"))
    out_specs = P("win", None, "chan", None)
    return jax.shard_map(local, mesh=mesh, in_specs=in_specs, out_specs=out_specs, check_vma=False)
```

profile of v0, /device:TPU:0, one launch (start us, length us, event | category | flops | bytes accessed | tf_op | source)
XLA Modules:
  0.0 373.9 jit_solution(17452706086946300186)
XLA Ops:
  6.5 0.0 all-gather.2.cloned.1.call-start
  6.5 0.7 fusion.12
  7.2 0.1 copy.13
  7.3 21.4 %cosine_convert_fusion = (bf16[384,3072]{1,0:T(8,128)(2,1)S(1)}, bf16[384,3072]{1,0:T(8,128)(2,1)}) fusion(s32[384]{0:T(512)S(1)} %iota_add_fusion), kind=kLoop, calls=%fused_computation.14 | loop fusion | flops 14155776 | bytes 4720128 | tf_op jit(solution)/shard_map/convert
  28.7 19.5 %while.1 = (s32[]{:T(128)}, bf16[4,3200,256]{2,1,0:T(8,128)(2,1)}, s32[4,3]{1,0:T(4,128)S(1)}, bf16[4,3072,256]{2,1,0:T(8,128)(2,1)}, s32[]{:T(128)}) while((s32[]{:T(128)}, bf16[4,3200,256]{2,1,0:T(8,128)(2,1)}, s32[4,3]{1,0:T(4,128)S(1)}, bf16[4,3072,256]{2,1,0:T(8,128)(2,1)}, s32[]{:T(128)}) %tuple.24), condition=%wide.while_cond, body=%wide.while_body.sunk | while | flops 2 | bytes 3146869 | solution.py:49
  28.7 0.6 fusion.17
  29.3 4.3 %dynamic-slice_dynamic-update-slice_fusion.2 = bf16[4,3072,256]{2,1,0:T(8,128)(2,1)} fusion(bf16[4,3072,256]{2,1,0:T(8,128)(2,1)} %get-tuple-element.76, s32[]{:T(128)S(6)} %copy.23, bf16[4,3200,256]{2,1,0:T(8,128)(2,1)} %get-tuple-element.79, s32[]{:T(128)} %bitcast.41, s32[]{:T(128)} %bitcast.42), kind=kLoop, calls=%fused_computation.clone.1 | loop fusion | bytes 3146756 | tf_op jit(solution)/shard_map/vmap()/gather
  33.6 0.6 fusion.17
  34.2 4.3 %dynamic-slice_dynamic-update-slice_fusion.2 = bf16[4,3072,256]{2,1,0:T(8,128)(2,1)} fusion(bf16[4,3072,256]{2,1,0:T(8,128)(2,1)} %get-tuple-element.76, s32[]{:T(128)S(6)} %copy.23, bf16[4,3200,256]{2,1,0:T(8,128)(2,1)} %get-tuple-element.79, s32[]{:T(128)} %bitcast.41, s32[]{:T(128)} %bitcast.42), kind=kLoop, calls=%fused_computation.clone.1 | loop fusion | bytes 3146756 | tf_op jit(solution)/shard_map/vmap()/gather
  38.4 0.6 fusion.17
  39.0 4.3 %dynamic-slice_dynamic-update-slice_fusion.2 = bf16[4,3072,256]{2,1,0:T(8,128)(2,1)} fusion(bf16[4,3072,256]{2,1,0:T(8,128)(2,1)} %get-tuple-element.76, s32[]{:T(128)S(6)} %copy.23, bf16[4,3200,256]{2,1,0:T(8,128)(2,1)} %get-tuple-element.79, s32[]{:T(128)} %bitcast.41, s32[]{:T(128)} %bitcast.42), kind=kLoop, calls=%fused_computation.clone.1 | loop fusion | bytes 3146756 | tf_op jit(solution)/shard_map/vmap()/gather
  43.3 0.6 fusion.17
  43.9 4.3 %dynamic-slice_dynamic-update-slice_fusion.2 = bf16[4,3072,256]{2,1,0:T(8,128)(2,1)} fusion(bf16[4,3072,256]{2,1,0:T(8,128)(2,1)} %get-tuple-element.76, s32[]{:T(128)S(6)} %copy.23, bf16[4,3200,256]{2,1,0:T(8,128)(2,1)} %get-tuple-element.79, s32[]{:T(128)} %bitcast.41, s32[]{:T(128)} %bitcast.42), kind=kLoop, calls=%fused_computation.clone.1 | loop fusion | bytes 3146756 | tf_op jit(solution)/shard_map/vmap()/gather
  48.2 0.0 copy-start.1
  48.2 8.1 %multiply_reduce_fusion = (f32[4,256]{1,0:T(4,128)S(1)}, f32[4,256,768]{2,1,0:T(8,128)S(1)}) fusion(bf16[4,3072,256]{2,1,0:T(8,128)(2,1)} %get-tuple-element.12, bf16[384,3072]{1,0:T(8,128)(2,1)} %get-tuple-element.36, bf16[384,3072]{1,0:T(8,128)(2,1)S(1)} %get-tuple-element.35), kind=kOutput, calls=%fused_computation.22 | convolution fusion | flops 4842847232 | bytes 14159872 | tf_op jit(solution)/shard_map/kl,wlc->wkc/dot_general | solution.py:52
  56.3 0.0 copy-done.1
  56.3 0.2 fusion.11
  56.5 0.4 reshape.12
  56.9 2.7 copy.15
  59.6 44.0 %all_to_all.18 = bf16[4,2,384,256]{3,1,0,2:T(2,128)(2,1)S(1)} all-to-all(bf16[4,2,384,256]{3,1,0,2:T(2,128)(2,1)S(1)} %copy.15), channel_id=1, replica_groups=mesh['chan'=4,'win'=8] {'win'}, dimensions={2} | all-to-all | bytes 3145728 | tf_op jit(solution)/shard_map/all_to_all | solution.py:57
  103.6 0.3 copy.16
  103.9 1.2 copy.17
  105.1 1.9 all_to_all.16
  107.0 0.0 all-gather.2.cloned.1.call-update
  107.0 0.0 copy-start
  107.0 69.1 %all-gather.2.cloned.1.call-done = bf16[32,2,48,1024]{3,0,2,1:T(8,128)(2,1)} async-done(((bf16[32,2,48,256]{3,0,2,1:T(8,128)(2,1)}), bf16[32,2,48,1024]{3,0,2,1:T(8,128)(2,1)}) %all-gather.2.cloned.1.call-update) | async-done | bytes 6291472 | tf_op jit(solution)/shard_map/all_gather | solution.py:58
  176.1 22.3 %fusion.9 = f32[48,256,1024]{2,1,0:T(8,128)} fusion(bf16[32,2,48,1024]{3,0,2,1:T(8,128)(2,1)} %all-gather.2.cloned.1.call-done, bf16[32,2,48,256]{3,0,2,1:T(8,128)(2,1)} %all_to_all.16), kind=kOutput, calls=%fused_computation.23 | convolution fusion | flops 805306368 | bytes 54263808 | tf_op jit(solution)/shard_map/wfi,wfj->fij/dot_general | solution.py:36
  198.4 0.0 copy-done
  198.4 21.2 %fusion.10 = f32[48,256,1024]{2,1,0:T(8,128)} fusion(bf16[32,2,48,1024]{3,0,2,1:T(8,128)(2,1)} %all-gather.2.cloned.1.call-done, bf16[32,2,48,256]{3,0,2,1:T(8,128)(2,1)S(1)} %copy-done), kind=kOutput, calls=%fused_computation.24 | convolution fusion | flops 805306368 | bytes 54263808 | tf_op jit(solution)/shard_map/wfi,wfj->fij/dot_general | solution.py:30
  219.6 33.2 %subtract_bitcast_fusion = f32[48,1,256,1024]{3,2,0,1:T(8,128)} fusion(f32[48,256,1024]{2,1,0:T(8,128)} %fusion.9, bf16[32,2,48,1024]{3,0,2,1:T(8,128)(2,1)} %all-gather.2.cloned.1.call-done, bf16[32,2,48,256]{3,0,2,1:T(8,128)(2,1)S(1)} %copy-done), kind=kOutput, calls=%fused_computation.4 | convolution fusion | flops 817889280 | bytes 104595456 | tf_op jit(solution)/shard_map/wfi,wfj->fij/dot_general | solution.py:39
  252.8 32.9 %add_bitcast_fusion = f32[48,1,256,1024]{3,2,0,1:T(8,128)} fusion(f32[48,256,1024]{2,1,0:T(8,128)} %fusion.10, bf16[32,2,48,1024]{3,0,2,1:T(8,128)(2,1)} %all-gather.2.cloned.1.call-done, bf16[32,2,48,256]{3,0,2,1:T(8,128)(2,1)S(1)} %copy-done), kind=kOutput, calls=%fused_computation.5 | convolution fusion | flops 817889280 | bytes 104595456 | tf_op jit(solution)/shard_map/wfi,wfj->fij/dot_general | solution.py:33
  285.6 48.5 %fusion = bf16[48,2,256,1024]{3,2,0,1:T(8,128)(2,1)} fusion(f32[48,1,256,1024]{3,2,0,1:T(8,128)} %subtract_bitcast_fusion, f32[48,1,256,1024]{3,2,0,1:T(8,128)} %add_bitcast_fusion), kind=kLoop, calls=%fused_computation.3 | loop fusion | flops 75497472 | bytes 150994944 | tf_op jit(solution)/shard_map/convert_element_type | solution.py:42
  334.1 32.9 %copy.18 = bf16[48,2,256,1024]{3,2,1,0:T(8,128)(2,1)} copy(bf16[48,2,256,1024]{3,2,0,1:T(8,128)(2,1)} %fusion) | data formatting | bytes 100663296 | tf_op jit(solution)/shard_map/convert_element_type | solution.py:42
  (9 shorter events, 0.0 us)
Async XLA Ops:
  6.5 169.5 %all-gather.2.cloned.1.call-start = ((), (), s32[]{:S(2)}) async-start(), calls=%async_computation.1 | async-start | bytes 7864320 | tf_op jit(solution)/shard_map/all_gather | solution.py:58
  48.2 8.1 %copy-start.1 = (s32[4,256]{1,0:T(4,128)S(1)}, s32[4,256]{1,0:T(4,128)}, u32[]{:S(2)}) copy-start(s32[4,256]{1,0:T(4,128)} %param.5) | copy-start | bytes 12292
  107.0 91.4 %copy-start = (bf16[32,2,48,256]{3,0,2,1:T(8,128)(2,1)S(1)}, bf16[32,2,48,256]{3,0,2,1:T(8,128)(2,1)}, u32[]{:S(2)}) copy-start(bf16[32,2,48,256]{3,0,2,1:T(8,128)(2,1)} %all_to_all.16) | copy-start | bytes 4718596
Sparse Core Ops, SparseCore 0:
  107.1 68.9 all-gather.1
where the time goes:
time: 374 us
  matrix products  118 us (32%)
  other arithmetic  70.8 us (19%)
  waiting for transfers between devices  69.1 us (18%)
  local copies, waits for them, and re-layouts  58.9 us (16%)
  blocking collectives  44 us (12%)
  between operations  13.5 us (4%)
    all_gather x1, waiting for transfers between devices, local(): lax.all_gather(bin_local, 'chan', axis=3, tiled=True)  69.1 us
    convert_element_type x1, other arithmetic, cross_spectra(): (jnp.stack([real_part, imag_part], 1) * stack_scale).astype(jnp.bfloat16)  48.5 us
    all_to_all x1, blocking collectives, local(): lax.all_to_all(spectra, 'win', split_axis=2, concat_axis=0, tiled=True)  44 us
    dot_general x1, matrix products, cross_spectra(): jnp.einsum('wfi,wfj->fij', real_mine, imag_other, preferred_element_type=...  33.2 us
    convert_element_type x1, local copies, waits for them, and re-layouts, cross_spectra(): (jnp.stack([real_part, imag_part], 1) * stack_scale).astype(jnp.bfloat16)  32.9 us
    dot_general x1, matrix products, cross_spectra(): jnp.einsum('wfi,wfj->fij', imag_mine, imag_other, preferred_element_type=...  32.9 us
    dot_general x1, matrix products, cross_spectra(): jnp.einsum('wfi,wfj->fij', imag_mine, real_other, preferred_element_type=...  22.3 us
    another operation x1, other arithmetic  21.4 us
  transfers between devices with their start and end apart: 1, of which 1 were waited for; matrix products, arithmetic and copies ran while one was open for 0% of the time, Pallas kernels for 0%

commit v1 on v0

v1 whole, which is shorter than its diff:
```python
import functools
import math

import jax
import jax.numpy as jnp
import ml_dtypes
import numpy as np
from jax import lax
from jax.experimental import pallas as pl
from jax.experimental.pallas import tpu as pltpu
from jax.sharding import PartitionSpec as P

F = 384
L = 3072
FIRST_BIN = 60
CHUNKS = 1

epsilon = 1e-05
VMEM_LIMIT = 56 * 1024 * 1024


def dft_table():
    sample_idx = np.arange(L, dtype=np.int64)
    bin_idx = FIRST_BIN + np.arange(F, dtype=np.int64)
    residue = bin_idx[:, None] * sample_idx[None, :] % L
    angles = residue.astype(np.float32) * np.float32(2.0 * math.pi / L)
    return np.concatenate([np.cos(angles), -np.sin(angles)], 0).astype(ml_dtypes.bfloat16)


def interleave(windows, bins):
    pair = 16 // (2 * windows)
    out = np.zeros((2 * windows * bins, 2 * windows * bins), np.float32)
    for f in range(bins):
        for p in range(2):
            for w in range(windows):
                row = ((f // pair * 2 + p) * pair + f % pair) * windows + w
                out[row, (w * 2 + p) * bins + f] = 1.0
    return out.astype(ml_dtypes.bfloat16)


def spectra_kernel(chunk_sizes, offsets_ref, table_ref, mix_ref, raw_ref, quality_ref, *refs):
    outs = refs[: len(chunk_sizes)]
    wide, window, white = refs[len(chunk_sizes) :]
    w = pl.program_id(0)
    windows = white.shape[0]
    seg, width = raw_ref.shape[1:]
    tile = 256

    wide[:seg] = raw_ref[0].astype(jnp.float32)
    shift_at = offsets_ref[w]
    coarse = shift_at // 8
    fine = shift_at - coarse * 8
    back = jnp.where(fine == 0, 0, 8 - fine)

    def cut(step, carry):
        start = pl.multiple_of((coarse + step * (tile // 8)) * 8, 8)
        rows = wide[pl.ds(start, tile + 8), :].reshape(tile // 8 + 1, 8, width)
        rolled = pltpu.roll(rows, back, 1)
        keep = lax.broadcasted_iota(jnp.int32, (tile // 8, 8, width), 1) < 8 - fine
        moved = jnp.where(keep, rolled[:-1], rolled[1:])
        window[pl.ds(pl.multiple_of(step * tile, tile), tile), :] = moved.reshape(tile, width).astype(jnp.bfloat16)
        return carry

    lax.fori_loop(0, L // tile, cut, 0)

    transform = jnp.dot(table_ref[...], window[...], preferred_element_type=jnp.float32)
    band_power = jnp.sum(transform * transform, axis=0, keepdims=True) / F
    whiten = lax.rsqrt(band_power + epsilon) * quality_ref[0].astype(jnp.float32)
    white[w] = (transform * whiten).astype(jnp.bfloat16)

    @pl.when(w == windows - 1)
    def _():
        pair = 16 // (2 * windows)
        bins = mix_ref.shape[0] // (2 * windows)
        share = sum(chunk_sizes)
        for block in range(F // bins):
            parts = [
                white[v, p * F + block * bins : p * F + (block + 1) * bins, :]
                for v in range(windows)
                for p in range(2)
            ]
            mixed = jnp.dot(mix_ref[...], jnp.concatenate(parts, 0), preferred_element_type=jnp.float32)
            mixed = mixed.astype(jnp.bfloat16)
            for g in range(bins // pair):
                group = block * (bins // pair) + g
                dest, at = group // share, group % share
                chunk = 0
                while at >= chunk_sizes[chunk]:
                    at -= chunk_sizes[chunk]
                    chunk += 1
                outs[chunk][dest, at] = mixed[g * 16 : (g + 1) * 16, :]


def spectra(raw, offsets, quality, dests, chunk_sizes):
    windows, seg, width = raw.shape
    bins = 256 // (2 * windows)
    table = jnp.asarray(dft_table())
    mix = jnp.asarray(interleave(windows, bins))
    grid_spec = pltpu.PrefetchScalarGridSpec(
        num_scalar_prefetch=1,
        grid=(windows,),
        in_specs=[
            pl.BlockSpec(table.shape, lambda w, _: (0, 0)),
            pl.BlockSpec(mix.shape, lambda w, _: (0, 0)),
            pl.BlockSpec((1, seg, width), lambda w, _: (w, 0, 0)),
            pl.BlockSpec((1, 1, width), lambda w, _: (w, 0, 0)),
        ],
        out_specs=[pl.BlockSpec((dests, size, 16, width), lambda w, _: (0, 0, 0, 0)) for size in chunk_sizes],
        scratch_shapes=[
            pltpu.VMEM((seg + 8, width), jnp.float32),
            pltpu.VMEM((L, width), jnp.bfloat16),
            pltpu.VMEM((windows, 2 * F, width), jnp.bfloat16),
        ],
    )
    return pl.pallas_call(
        functools.partial(spectra_kernel, chunk_sizes),
        grid_spec=grid_spec,
        out_shape=[jax.ShapeDtypeStruct((dests, size, 16, width), jnp.bfloat16) for size in chunk_sizes],
        compiler_params=pltpu.CompilerParams(vmem_limit_bytes=VMEM_LIMIT, dimension_semantics=("arbitrary",)),
        cost_estimate=pl.CostEstimate(
            flops=2 * windows * 2 * F * L * width, bytes_accessed=2 * windows * seg * width + 4 * F * L, transcendentals=0
        ),
        name="spectra",
    )(offsets, table, mix, raw, quality.reshape(windows, 1, width))


def stack_kernel(windows, scale, mine_ref, all_ref, *refs):
    out_ref = refs[-1]
    pair = 16 // (2 * windows)
    sources, _, rows, width = mine_ref.shape
    depth = sources * rows
    mine = mine_ref[:, 0].astype(jnp.float32)
    turned = jnp.concatenate([mine[:, 8:], -mine[:, :8]], 1)
    real_left = mine.reshape(depth, width).T.astype(jnp.bfloat16)
    imag_left = turned.reshape(depth, width).T.astype(jnp.bfloat16)
    bin_of = lax.broadcasted_iota(jnp.int32, (width, depth), 1) % 8 // windows
    lefts = []
    for b in range(pair):
        for left in (real_left, imag_left):
            lefts.append(jnp.where(bin_of == b, left, jnp.zeros_like(left)))
    for j in range(all_ref.shape[0]):
        right = all_ref[j, :, 0].reshape(depth, width)
        for n, left in enumerate(lefts):
            product = jnp.dot(left, right, preferred_element_type=jnp.float32)
            out_ref[n // 2, n % 2, :, j * width : (j + 1) * width] = (product * scale).astype(jnp.bfloat16)


def stack(mine, everyone, into, first_group, share, windows):
    sources, groups, rows, width = mine.shape
    blocks = everyone.shape[0]
    pair = 16 // (2 * windows)
    scale = 1.0 / math.sqrt(sources * windows)
    operands = [mine, everyone]
    in_specs = [
        pl.BlockSpec((sources, 1, rows, width), lambda g: (0, g, 0, 0)),
        pl.BlockSpec((blocks, sources, 1, rows, width), lambda g: (0, 0, g, 0, 0)),
    ]
    aliases = {}
    if into is not None:
        operands.append(into)
        in_specs.append(pl.BlockSpec(memory_space=pl.ANY))
        aliases = {2: 0}
    return pl.pallas_call(
        functools.partial(stack_kernel, windows, scale),
        grid=(groups,),
        in_specs=in_specs,
        out_specs=pl.BlockSpec((pair, 2, width, blocks * width), lambda g: (first_group + g, 0, 0, 0)),
        out_shape=jax.ShapeDtypeStruct((share * pair, 2, width, blocks * width), jnp.bfloat16),
        input_output_aliases=aliases,
        compiler_params=pltpu.CompilerParams(vmem_limit_bytes=VMEM_LIMIT, dimension_semantics=("arbitrary",)),
        cost_estimate=pl.CostEstimate(
            flops=8 * groups * pair * sources * rows * width * width * blocks,
            bytes_accessed=4 * groups * pair * width * blocks * width,
            transcendentals=0,
        ),
        name="stack",
    )(*operands)


def local(chunks, dests, raw, offsets, quality):
    windows = raw.shape[0]
    pair = 16 // (2 * windows)
    share = F // (dests * pair)
    while share % chunks:
        chunks -= 1
    chunk_sizes = [share // chunks] * chunks
    pieces = spectra(raw, offsets, quality, dests, chunk_sizes)
    out = None
    for chunk, piece in enumerate(pieces):
        mine = lax.all_to_all(piece, "win", split_axis=0, concat_axis=0, tiled=True)
        everyone = lax.all_gather(mine, "chan", axis=0, tiled=False)
        out = stack(mine, everyone, out, sum(chunk_sizes[:chunk]), share, windows)
    return out


def solution(mesh):
    in_specs = (P("win", None, "chan"), P("win"), P("win", "chan"))
    out_specs = P("win", None, "chan", None)
    run = functools.partial(local, CHUNKS, mesh.shape["win"])
    return jax.shard_map(run, mesh=mesh, in_specs=in_specs, out_specs=out_specs, check_vma=False)
```

time: 374 us -> 171 us (0.46)
  matrix products: 118 us -> 0 us
  other arithmetic: 70.8 us -> 0 us
  local copies, waits for them, and re-layouts: 58.9 us -> 1.28 us
  Pallas kernels: 0 us -> 41.8 us
    dot_general x5 -> x0, matrix products: 118 us -> none  [the longest x1 33.2 us: cross_spectra(): jnp.einsum('wfi,wfj->fij', real_mine, imag_other, preferred_element_type=...]
    convert_element_type x2 -> x0, other arithmetic: 48.7 us -> none  [the longest x1 48.5 us: cross_spectra(): (jnp.stack([real_part, imag_part], 1) * stack_scale).astype(jnp.bfloat16)]
    pallas_call x0 -> x2, Pallas kernels: none -> 41.8 us  [the longest x1 28.4 us: stack(): pl.pallas_call(functools.partial(stack_kernel, windows, scale), grid=(gro...]
    convert_element_type x1 -> x0, local copies, waits for them, and re-layouts: 32.9 us -> none  [cross_spectra(): (jnp.stack([real_part, imag_part], 1) * stack_scale).astype(jnp.bfloat16)]
    another operation x1 -> x0, other arithmetic: 21.4 us -> none
    gather x12 -> x0, local copies, waits for them, and re-layouts: 19.5 us -> none
where the time goes in v1:
time: 171 us; the launch traced here: 170 us
  waiting for transfers between devices  69.2 us (40%)
  blocking collectives  44.3 us (26%)
  Pallas kernels  41.8 us (24%)
  between operations  13.4 us (8%)
    all_gather x1, waiting for transfers between devices, local(): everyone = lax.all_gather(mine, 'chan', axis=0, tiled=False)  69.2 us
    all_to_all x1, blocking collectives, local(): mine = lax.all_to_all(piece, 'win', split_axis=0, concat_axis=0, tiled=True)  44.3 us
    pallas_call x1, Pallas kernels, stack(): pl.pallas_call(functools.partial(stack_kernel, windows, scale), grid=(gro...  28.4 us
    pallas_call x1, Pallas kernels, spectra(): pl.pallas_call(functools.partial(spectra_kernel, chunk_sizes), grid_spec=...  13.4 us
  transfers between devices with their start and end apart: 1, of which 1 were waited for; matrix products, arithmetic and copies ran while one was open for 0% of the time, Pallas kernels for 0%

profile of v1, /device:TPU:0, one launch (start us, length us, event | category | flops | bytes accessed | tf_op | source)
XLA Modules:
  0.0 169.9 jit_solution(8199329906514264583)
XLA Ops:
  6.5 0.0 all-gather.3.cloned.1.call-start
  6.5 1.3 reshape.3.quality_ref
  7.8 13.4 %spectra.1 = bf16[8,24,16,256]{3,2,1,0:T(8,128)(2,1)} custom-call(s32[4]{0:T(128)} %offsets_ref.1, bf16[768,3072]{1,0:T(8,128)(2,1)} %constant.4.clone.table_ref, bf16[256,256]{1,0:T(8,128)(2,1)} %constant.5.clone.mix_ref, bf16[4,3200,256]{2,1,0:T(8,128)(2,1)} %raw_ref.1, s32[4,1,256]{2,1,0:T(1,128)} %reshape.3.quality_ref), custom_call_target="tpu_custom_call" | custom-call | flops 4831838208 | bytes 11272192 | tf_op jit(solution)/shard_map/spectra/pallas_call | solution.py:115
  21.2 44.3 %all_to_all.5.mine_ref = bf16[8,24,16,256]{3,2,1,0:T(8,128)(2,1)} all-to-all(bf16[8,24,16,256]{3,2,1,0:T(8,128)(2,1)} %spectra.1), channel_id=1, replica_groups=mesh['chan'=4,'win'=8] {'win'}, dimensions={0} | all-to-all | bytes 3145728 | tf_op jit(solution)/shard_map/all_to_all | solution.py:190
  65.5 0.0 all-gather.3.cloned.1.call-update
  65.5 69.2 %all-gather.3.cloned.1.call-done = bf16[32,24,16,256]{3,2,1,0:T(8,128)(2,1)} async-done(((bf16[8,24,16,256]{3,2,1,0:T(8,128)(2,1)}), bf16[32,24,16,256]{3,2,1,0:T(8,128)(2,1)}) %all-gather.3.cloned.1.call-update) | async-done | bytes 6291472 | tf_op jit(solution)/shard_map/all_gather | solution.py:191
  134.7 28.4 %stack.1 = bf16[48,2,256,1024]{3,2,1,0:T(8,128)(2,1)} custom-call(bf16[8,24,16,256]{3,2,1,0:T(8,128)(2,1)} %all_to_all.5.mine_ref, bf16[4,8,24,16,256]{4,3,2,1,0:T(8,128)(2,1)} %bitcast.1), custom_call_target="tpu_custom_call" | custom-call | flops 12884901888 | bytes 50331648 | tf_op jit(solution)/shard_map/stack/pallas_call | solution.py:163
Async XLA Ops:
  6.5 128.2 %all-gather.3.cloned.1.call-start = ((), (), s32[]{:S(2)}) async-start(), calls=%async_computation.1 | async-start | bytes 7864320 | tf_op jit(solution)/shard_map/all_gather | solution.py:191
Sparse Core Ops, SparseCore 0:
  65.6 69.0 all-gather.2

commit v2 on v0

v2 whole, which is shorter than its diff:
```python
import functools
import math

import jax
import jax.numpy as jnp
import ml_dtypes
import numpy as np
from jax import lax
from jax.experimental import pallas as pl
from jax.experimental.pallas import tpu as pltpu
from jax.sharding import PartitionSpec as P

F = 384
L = 3072
FIRST_BIN = 60
CHUNK_WEIGHTS = (1, 1, 1)
STEP_GROUPS = 2

epsilon = 1e-05
MIB = 1024 * 1024


def dft_table():
    sample_idx = np.arange(L, dtype=np.int64)
    bin_idx = FIRST_BIN + np.arange(F, dtype=np.int64)
    residue = bin_idx[:, None] * sample_idx[None, :] % L
    angles = residue.astype(np.float32) * np.float32(2.0 * math.pi / L)
    return np.concatenate([np.cos(angles), -np.sin(angles)], 0).astype(ml_dtypes.bfloat16)


def interleave(windows, bins):
    pair = 16 // (2 * windows)
    out = np.zeros((2 * windows * bins, 2 * windows * bins), np.float32)
    for f in range(bins):
        for p in range(2):
            for w in range(windows):
                row = ((f // pair * 2 + p) * pair + f % pair) * windows + w
                out[row, (w * 2 + p) * bins + f] = 1.0
    return out.astype(ml_dtypes.bfloat16)


def cut(raw_ref, slot, shift_at, window_ref):
    width = raw_ref.shape[2]
    spare = raw_ref.shape[1] - L
    tile = 256
    base = jnp.minimum(shift_at // 16, (spare - 16) // 16) * 16
    rest = shift_at - base
    whole = rest // 8
    fine = rest - whole * 8
    back = jnp.where(fine == 0, 0, 8 - fine)
    keep = lax.broadcasted_iota(jnp.int32, (tile // 8, 8, width), 1) < 8 - fine
    count = tile // 8
    for step in range(L // tile):
        start = pl.multiple_of(base + step * tile, 16)
        rows = raw_ref[slot, pl.ds(start, tile + 16), :].astype(jnp.float32).reshape(count + 2, 8, width)
        rolled = pltpu.roll(rows, back, 1)
        upper = jnp.where(whole == 0, rolled[1 : count + 1], rolled[2:])
        lower = jnp.where(whole == 0, rolled[:count], jnp.where(whole == 1, rolled[1 : count + 1], rolled[2:]))
        moved = jnp.where(keep, lower, upper)
        window_ref[step * tile : (step + 1) * tile, :] = moved.reshape(tile, width).astype(jnp.bfloat16)


def spectra_kernel(offsets_ref, table_ref, mix_ref, raw_ref, quality_ref, keep_ref, give_ref, *scratch):
    white, mixed = scratch[:2]
    cuts = scratch[2:]
    windows, _, width = raw_ref.shape
    for w in range(windows):
        cut(raw_ref, w, offsets_ref[w], cuts[w])
        transform = jnp.dot(table_ref[...], cuts[w][...], preferred_element_type=jnp.float32)
        band_power = jnp.sum(transform * transform, axis=0, keepdims=True) / F
        usable = quality_ref[w : w + 1, :].astype(jnp.float32)
        white[w] = (transform * (lax.rsqrt(band_power + epsilon) * usable)).astype(jnp.bfloat16)

    pair = 16 // (2 * windows)
    bins = mix_ref.shape[0] // (2 * windows)
    groups = bins // pair
    for block in range(F // bins):
        parts = [
            white[v, p * F + block * bins : p * F + (block + 1) * bins, :] for v in range(windows) for p in range(2)
        ]
        product = jnp.dot(mix_ref[...], jnp.concatenate(parts, 0), preferred_element_type=jnp.float32)
        mixed[block * groups : (block + 1) * groups] = product.astype(jnp.bfloat16).reshape(groups, 16, width)
    me = lax.axis_index("win")
    chip, core = me // 2, me % 2
    chips, share = keep_ref.shape[:2]
    for k in range(chips):
        at = (chip ^ k) * 2 * share
        keep_ref[k] = mixed[pl.ds(at + core * share, share)]
        give_ref[k] = mixed[pl.ds(at + (1 - core) * share, share)]


def in_vmem(count):
    return [pl.BlockSpec(memory_space=pltpu.VMEM)] * count


def spectra(raw, offsets, quality, table, mix, dests):
    windows, _, width = raw.shape
    groups = F * 2 * windows // 16
    blocks = (dests // 2, groups // dests, 16, width)
    return pl.pallas_call(
        spectra_kernel,
        in_specs=[pl.BlockSpec(memory_space=pltpu.SMEM), *in_vmem(4)],
        out_specs=in_vmem(2),
        scratch_shapes=[
            pltpu.VMEM((windows, 2 * F, width), jnp.bfloat16),
            pltpu.VMEM((groups, 16, width), jnp.bfloat16),
            *[pltpu.VMEM((L, width), jnp.bfloat16)] * windows,
        ],
        out_shape=[jax.ShapeDtypeStruct(blocks, jnp.bfloat16)] * 2,
        compiler_params=pltpu.CompilerParams(vmem_limit_bytes=24 * MIB),
        cost_estimate=pl.CostEstimate(
            flops=2 * windows * 2 * F * L * width, bytes_accessed=2 * windows * raw.shape[1] * width + 4 * F * L, transcendentals=0
        ),
        name="spectra",
    )(offsets, table, mix, raw, quality)


def join_kernel(moves, *refs):
    out_ref = refs[-1]
    groups = out_ref.shape[1]
    to = 0
    for i, at, source, count in moves:
        out_ref[to : to + count] = refs[i][source : source + count, at : at + groups]
        to += count


def join(views, groups):
    arrays, moves = [], []
    for x, *where in views:
        known = [i for i, y in enumerate(arrays) if y is x]
        if not known:
            arrays.append(x)
        moves.append((known[0] if known else len(arrays) - 1, *where))
    shape = (sum(move[3] for move in moves), groups, *arrays[0].shape[2:])
    return pl.pallas_call(
        functools.partial(join_kernel, moves),
        in_specs=in_vmem(len(arrays)),
        out_specs=in_vmem(1)[0],
        out_shape=jax.ShapeDtypeStruct(shape, arrays[0].dtype),
        compiler_params=pltpu.CompilerParams(vmem_limit_bytes=12 * MIB),
        cost_estimate=pl.CostEstimate(flops=0, bytes_accessed=4 * math.prod(shape), transcendentals=0),
        name="join",
    )(*arrays)


def view(ref, group, at, sources):
    return ref[sources[0] : sources[1], group - at].reshape(-1, ref.shape[-1])


def turn_kernel(first_group, views, *refs):
    out_ref = refs[-1]
    _, _, width, depth = out_ref.shape

    def body(g, carry):
        x = jnp.concatenate([view(refs[i], first_group + g, *where) for i, where in enumerate(views)], 0)
        by_part = x.astype(jnp.float32).reshape(depth // 16, 16, width)
        turned = jnp.concatenate([by_part[:, 8:], -by_part[:, :8]], 1)
        out_ref[g, 0] = by_part.reshape(depth, width).T.astype(jnp.bfloat16)
        out_ref[g, 1] = turned.reshape(depth, width).T.astype(jnp.bfloat16)
        return carry

    lax.fori_loop(0, out_ref.shape[0], body, 0)


def turn(items, first_group, groups):
    rows, width = items[0][0].shape[2:]
    depth = sum(sources[1] - sources[0] for _, _, sources in items) * rows
    return pl.pallas_call(
        functools.partial(turn_kernel, first_group, [item[1:] for item in items]),
        in_specs=in_vmem(len(items)),
        out_specs=in_vmem(1)[0],
        out_shape=jax.ShapeDtypeStruct((groups, 2, width, depth), jnp.bfloat16),
        compiler_params=pltpu.CompilerParams(vmem_limit_bytes=12 * MIB),
        cost_estimate=pl.CostEstimate(flops=0, bytes_accessed=8 * groups * width * depth, transcendentals=0),
        name="turn",
    )(*[item[0] for item in items])


def closed_walk(i, members):
    return jnp.where(i < members // 2, i, members - 1 - i + members // 2)


def stack_kernel(windows, scale, first_group, layout, left_ref, *refs):
    out_ref = refs[-1]
    pair = 16 // (2 * windows)
    width, depth = left_ref.shape[2:]
    step_groups = out_ref.shape[0] // pair
    members = len(layout)
    where = closed_walk(lax.axis_index("chan"), members)
    bin_of = lax.broadcasted_iota(jnp.int32, (width, depth), 1) % 8 // windows
    masks = [jnp.where(bin_of == b, 1.0, 0.0).astype(jnp.bfloat16) for b in range(pair)]
    for s in range(step_groups):
        g = pl.program_id(0) * step_groups + s
        sides = [left_ref[g, part] for part in range(2)]
        for step, items in layout:
            right = jnp.concatenate([view(refs[i], first_group + g, *item) for i, item in items], 0)
            column = closed_walk(lax.rem(where + (step + members), members), members)
            columns = pl.ds(pl.multiple_of(column * width, width), width)
            for b in range(pair):
                for part in range(2):
                    product = jnp.dot(sides[part] * masks[b], right, preferred_element_type=jnp.float32)
                    out_ref[s * pair + b, part, :, columns] = (product * scale).astype(jnp.bfloat16)


def stack(left, steps, into, first_group, bins, windows, sources):
    members = len(steps)
    groups, _, width, depth = left.shape
    pair = 16 // (2 * windows)
    step_groups = max(n for n in range(1, STEP_GROUPS + 1) if groups % n == 0 and first_group % n == 0)
    operands, layout = [left], []
    for step, items in steps:
        layout.append((step, [(len(operands) - 1 + i, item[1:]) for i, item in enumerate(items)]))
        operands += [item[0] for item in items]
    in_specs = in_vmem(len(operands))
    aliases = {}
    if into is not None:
        aliases = {len(operands): 0}
        operands.append(into)
        in_specs.append(pl.BlockSpec(memory_space=pl.ANY))
    block = (step_groups * pair, 2, width, members * width)
    return pl.pallas_call(
        functools.partial(stack_kernel, windows, 1.0 / math.sqrt(sources), first_group, layout),
        grid=(groups // step_groups,),
        in_specs=in_specs,
        out_specs=pl.BlockSpec(block, lambda g: (first_group // step_groups + g, 0, 0, 0)),
        out_shape=jax.ShapeDtypeStruct((bins, 2, width, members * width), jnp.bfloat16),
        input_output_aliases=aliases,
        compiler_params=pltpu.CompilerParams(vmem_limit_bytes=24 * MIB, dimension_semantics=("arbitrary",)),
        cost_estimate=pl.CostEstimate(
            flops=4 * groups * pair * depth * width * width * members,
            bytes_accessed=4 * groups * pair * width * members * width,
            transcendentals=0,
        ),
        name="stack",
    )(*operands)


def after(arrays, *earlier):
    return list(lax.optimization_barrier((tuple(arrays), earlier))[0])


def ring_gather(x, members, before_last=None):
    ring = [i if i < members // 2 else members - 1 - i + members // 2 for i in range(members)]
    ahead = [(ring[i], ring[(i + 1) % members]) for i in range(members)]
    back = [(b, a) for a, b in ahead]
    left = right = x
    blocks = [(0, [x])]
    for step in range(1, (members + 1) // 2):
        left = lax.ppermute(left, "chan", ahead)
        right = lax.ppermute(right, "chan", back)
        blocks += [(-step, [left]), (step, [right])]
    if members % 2 == 0:
        cut_at = x.shape[0] // 2
        if before_last is not None:
            left, right = after((left, right), before_last)
        first = lax.ppermute(left[:cut_at], "chan", ahead)
        second = lax.ppermute(right[cut_at:], "chan", back)
        blocks.append((members // 2, [first, second]))
    return blocks


def neighbours(blocks):
    return [array for _, arrays in blocks[1:3] for array in arrays]


def chunk_starts(share):
    total, starts, seen = sum(CHUNK_WEIGHTS), [0], 0
    for weight in CHUNK_WEIGHTS:
        seen += weight
        starts.append(round(share * seen / total))
    return starts


def local(dests, members, raw, offsets, quality):
    windows = raw.shape[0]
    pair = 16 // (2 * windows)
    bins = F // dests
    share = bins // pair
    chips = dests // 2
    assert chips & (chips - 1) == 0
    starts = chunk_starts(share)
    chunks = list(zip(starts[:-1], starts[1:]))
    table = jnp.asarray(dft_table())
    mix = jnp.asarray(interleave(windows, 256 // (2 * windows)))

    keep, give = spectra(raw, offsets, quality, table, mix, dests)
    other = lax.ppermute(give, "win", [(i, i ^ 1) for i in range(dests)])
    own = join([(keep, 0, 0, 1), (other, 0, 0, 1)], share)
    own_blocks = ring_gather(own, members)

    arrived, first = [], None
    for start, stop in chunks:
        held = [[(keep, start, k, 1), (other, start, k, 1)] for k in range(chips)]
        across, sources = chips // 2, 2
        while across:
            sent = join(sum(held[across : 2 * across], []), stop - start)
            if first is not None and across == chips // 2:
                sent = after([sent], first)[0]
            elif first is not None and start == 0:
                sent = after([sent], *neighbours(own_blocks))[0]
            came = lax.ppermute(sent, "win", [(i, i ^ (2 * across)) for i in range(dests)])
            if across == chips // 2:
                first = came
            for k in range(across):
                held[k].append((came, 0, k * sources, sources))
            across, sources = across // 2, 2 * sources
        arrived.append(join(held[0][2:], stop - start))

    out = None
    for (start, stop), far in zip(chunks, arrived):
        blocks = ring_gather(far, members, out)
        steps = []
        for (step, own_arrays), (_, arrays) in zip(own_blocks, blocks):
            views = [(x, 0, (0, x.shape[0])) for x in own_arrays] + [(x, start, (0, x.shape[0])) for x in arrays]
            steps.append((step, views))
        left = turn(steps[0][1], start, stop - start)
        out = stack(left, steps, out, start, bins, windows, dests * windows)
    return out


def solution(mesh):
    in_specs = (P("win", None, "chan"), P("win"), P("win", "chan"))
    out_specs = P("win", None, "chan", None)
    run = functools.partial(local, mesh.shape["win"], mesh.shape["chan"])
    return jax.shard_map(run, mesh=mesh, in_specs=in_specs, out_specs=out_specs, check_vma=False)
```

time: 374 us -> 108 us (0.29)
  matrix products: 118 us -> 0 us
  other arithmetic: 70.8 us -> 0 us
  local copies, waits for them, and re-layouts: 58.9 us -> 7.55 us
  blocking collectives: 44 us -> 0 us
  Pallas kernels: 0 us -> 33.1 us
  waiting for transfers between devices: 69.1 us -> 36 us
  starting transfers between devices: 0.01 us -> 30.9 us
  between operations: 13.5 us -> 0.16 us
    dot_general x5 -> x0, matrix products: 118 us -> none  [the longest x1 33.2 us: cross_spectra(): jnp.einsum('wfi,wfj->fij', real_mine, imag_other, preferred_element_type=...]
    all_gather x1 -> x0, waiting for transfers between devices: 69.1 us -> none  [local(): lax.all_gather(bin_local, 'chan', axis=3, tiled=True)]
    convert_element_type x2 -> x0, other arithmetic: 48.7 us -> none  [the longest x1 48.5 us: cross_spectra(): (jnp.stack([real_part, imag_part], 1) * stack_scale).astype(jnp.bfloat16)]
    all_to_all x1 -> x0, blocking collectives: 44 us -> none  [local(): lax.all_to_all(spectra, 'win', split_axis=2, concat_axis=0, tiled=True)]
    ppermute x0 -> x23, waiting for transfers between devices: none -> 36 us  [the longest x6 23.8 us: local(): lax.ppermute(sent, 'win', [(i, i ^ 2 * across) for i in range(dests)])]
    pallas_call x0 -> x17, Pallas kernels: none -> 33.1 us  [the longest x3 23.7 us: stack(): pl.pallas_call(functools.partial(stack_kernel, windows, 1.0 / math.sqrt(s...]
    convert_element_type x1 -> x0, local copies, waits for them, and re-layouts: 32.9 us -> none  [cross_spectra(): (jnp.stack([real_part, imag_part], 1) * stack_scale).astype(jnp.bfloat16)]
    ppermute x0 -> x23, starting transfers between devices: none -> 30.9 us  [the longest x6 10.5 us: local(): lax.ppermute(sent, 'win', [(i, i ^ 2 * across) for i in range(dests)])]
  transfers between devices with their start and end apart: 1 -> 23, of which waited for: 1 -> 13; matrix products, arithmetic and copies ran while one was open for 0% -> 0% of each run, Pallas kernels for 0% -> 17%
where the time goes in v2:
time: 108 us
  waiting for transfers between devices  36 us (33%)
  Pallas kernels  33.1 us (31%)
  starting transfers between devices  30.9 us (29%)
  local copies, waits for them, and re-layouts  7.55 us (7%)
    ppermute x6, waiting for transfers between devices, local(): lax.ppermute(sent, 'win', [(i, i ^ 2 * across) for i in range(dests)])  23.8 us
    pallas_call x3, Pallas kernels, stack(): pl.pallas_call(functools.partial(stack_kernel, windows, 1.0 / math.sqrt(s...  23.7 us
    ppermute x6, starting transfers between devices, local(): lax.ppermute(sent, 'win', [(i, i ^ 2 * across) for i in range(dests)])  10.5 us
    unnamed x10, local copies, waits for them, and re-layouts  7.44 us
    pallas_call x1, Pallas kernels, spectra(): pl.pallas_call(spectra_kernel, in_specs=[pl.BlockSpec(memory_space=pltpu....  6.72 us
    ppermute x4, starting transfers between devices, ring_gather(): left = lax.ppermute(left, 'chan', ahead)  6.53 us
    ppermute x4, starting transfers between devices, ring_gather(): first = lax.ppermute(left[:cut_at], 'chan', ahead)  6.24 us
    ppermute x4, waiting for transfers between devices, ring_gather(): first = lax.ppermute(left[:cut_at], 'chan', ahead)  4.47 us
  transfers between devices with their start and end apart: 23, of which 13 were waited for; matrix products, arithmetic and copies ran while one was open for 0% of the time, Pallas kernels for 17%

profile of v2, /device:TPU:0, one launch (start us, length us, event | category | flops | bytes accessed | tf_op | source)
XLA Modules:
  0.0 107.8 jit_solution(4539820129175056351)
XLA Ops:
  0.0 0.0 copy-start
  0.0 2.9 %copy-done = bf16[4,3200,256]{2,1,0:T(8,128)(2,1)S(1)} copy-done((bf16[4,3200,256]{2,1,0:T(8,128)(2,1)S(1)}, bf16[4,3200,256]{2,1,0:T(8,128)(2,1)}, u32[]{:S(2)}) %copy-start) | copy-done | bytes 6553624
  2.9 0.0 copy-start.1
  2.9 0.7 copy-done.1
  3.5 0.0 copy-start.2
  3.5 0.7 copy-done.2
  4.2 0.0 copy-start.3
  4.2 2.3 %copy-done.3 = bf16[768,3072]{1,0:T(8,128)(2,1)S(1)} copy-done((bf16[768,3072]{1,0:T(8,128)(2,1)S(1)}, bf16[768,3072]{1,0:T(8,128)(2,1)}, u32[]{:S(2)}) %copy-start.3) | copy-done | bytes 4718616
  6.5 0.0 copy-start.4
  6.5 0.9 copy-done.4
  7.4 6.7 %spectra.1 = (bf16[4,24,16,256]{3,2,1,0:T(8,128)(2,1)S(1)}, bf16[4,24,16,256]{3,2,1,0:T(8,128)(2,1)S(1)}) custom-call(s32[4]{0:T(128)S(1)} %copy-done.2, bf16[768,3072]{1,0:T(8,128)(2,1)S(1)} %copy-done.3, bf16[256,256]{1,0:T(8,128)(2,1)S(1)} %copy-done.4, bf16[4,3200,256]{2,1,0:T(8,128)(2,1)S(1)} %copy-done, s32[4,256]{1,0:T(4,128)S(1)} %copy-done.1), custom_call_target="tpu_custom_call" | custom-call | flops 4831838208 | bytes 11272192 | tf_op jit(solution)/shard_map/spectra/pallas_call | solution.py:100
  14.2 0.5 collective-permute-start
  14.7 1.9 %collective-permute-done.refs_1_ = bf16[4,24,16,256]{3,2,1,0:T(8,128)(2,1)S(1)} collective-permute-done((bf16[4,24,16,256]{3,2,1,0:T(8,128)(2,1)S(1)}, bf16[4,24,16,256]{3,2,1,0:T(8,128)(2,1)S(1)}, u32[]{:S(2)}, u32[]{:S(2)}) %collective-permute-start) | collective-permute-done | bytes 786464 | tf_op jit(solution)/shard_map/ppermute | solution.py:287
  16.6 2.9 %collective-permute-start.5 = (bf16[2,24,16,256]{3,2,1,0:T(8,128)(2,1)S(1)}, bf16[2,24,16,256]{3,2,1,0:T(8,128)(2,1)S(1)}, u32[]{:S(2)}, u32[]{:S(2)}) collective-permute-start(bf16[2,24,16,256]{3,2,1,0:T(8,128)(2,1)S(1)} %join.10.refs_0_), channel_id=1, source_target_pairs={{0,8},{8,24},{24,16},{16,0},{1,9},{9,25},{25,17},{17,1},{2,10},{10... | collective-permute-start | bytes 1179656 | tf_op jit(solution)/shard_map/ppermute | solution.py:249
  19.5 0.1 collective-permute-start.7
  19.7 3.1 %collective-permute-start.1 = (bf16[4,8,16,256]{3,2,1,0:T(8,128)(2,1)S(1)}, bf16[4,8,16,256]{3,2,1,0:T(8,128)(2,1)S(1)}, u32[]{:S(2)}, u32[]{:S(2)}) collective-permute-start(bf16[4,8,16,256]{3,2,1,0:T(8,128)(2,1)S(1)} %join.13), channel_id=1, source_target_pairs={{0,4},{1,5},{2,6},{3,7},{4,0},{5,1},{6,2},{7,3},{8,12},{9,13},{10,... | collective-permute-start | bytes 786440 | tf_op jit(solution)/shard_map/ppermute | solution.py:301
  22.8 11.7 %collective-permute-done.1.refs_2_.refs_0_ = bf16[4,8,16,256]{3,2,1,0:T(8,128)(2,1)S(1)} collective-permute-done((bf16[4,8,16,256]{3,2,1,0:T(8,128)(2,1)S(1)}, bf16[4,8,16,256]{3,2,1,0:T(8,128)(2,1)S(1)}, u32[]{:S(2)}, u32[]{:S(2)}) %collective-permute-start.1) | collective-permute-done | bytes 262176 | tf_op jit(solution)/shard_map/ppermute | solution.py:301
  34.4 0.0 collective-permute-done.5.refs_2_
  34.5 0.0 collective-permute-done.7.refs_4_
  34.5 0.8 collective-permute-start.14
  35.3 3.4 %collective-permute-start.2 = (bf16[4,8,16,256]{3,2,1,0:T(8,128)(2,1)S(1)}, bf16[4,8,16,256]{3,2,1,0:T(8,128)(2,1)S(1)}, u32[]{:S(2)}, u32[]{:S(2)}) collective-permute-start(bf16[4,8,16,256]{3,2,1,0:T(8,128)(2,1)S(1)} %join.12), channel_id=1, source_target_pairs={{0,4},{1,5},{2,6},{3,7},{4,0},{5,1},{6,2},{7,3},{8,12},{9,13},{10,... | collective-permute-start | bytes 786440 | tf_op jit(solution)/shard_map/ppermute | solution.py:301
  38.7 8.3 %collective-permute-done.14.refs_1_ = bf16[4,8,16,256]{3,2,1,0:T(8,128)(2,1)S(1)} collective-permute-done((bf16[4,8,16,256]{3,2,1,0:T(8,128)(2,1)S(1)}, bf16[4,8,16,256]{3,2,1,0:T(8,128)(2,1)S(1)}, u32[]{:S(2)}, u32[]{:S(2)}) %collective-permute-start.14) | collective-permute-done | bytes 262176 | tf_op jit(solution)/shard_map/ppermute | solution.py:301
  47.1 1.5 %collective-permute-start.15 = (bf16[6,8,16,256]{3,2,1,0:T(8,128)(2,1)S(1)}, bf16[6,8,16,256]{3,2,1,0:T(8,128)(2,1)S(1)}, u32[]{:S(2)}, u32[]{:S(2)}) collective-permute-start(bf16[6,8,16,256]{3,2,1,0:T(8,128)(2,1)S(1)} %join.19.refs_1_), channel_id=1, source_target_pairs={{0,8},{8,24},{24,16},{16,0},{1,9},{9,25},{25,17},{17,1},{2,10},{10... | collective-permute-start | bytes 1179656 | tf_op jit(solution)/shard_map/ppermute | solution.py:249
  48.6 0.5 collective-permute-start.16
  49.2 1.4 %collective-permute-done.2.refs_2_.refs_0_ = bf16[4,8,16,256]{3,2,1,0:T(8,128)(2,1)S(1)} collective-permute-done((bf16[4,8,16,256]{3,2,1,0:T(8,128)(2,1)S(1)}, bf16[4,8,16,256]{3,2,1,0:T(8,128)(2,1)S(1)}, u32[]{:S(2)}, u32[]{:S(2)}) %collective-permute-start.2) | collective-permute-done | bytes 262176 | tf_op jit(solution)/shard_map/ppermute | solution.py:301
  50.6 0.3 collective-permute-start.11
  50.9 2.8 %collective-permute-start.3 = (bf16[4,8,16,256]{3,2,1,0:T(8,128)(2,1)S(1)}, bf16[4,8,16,256]{3,2,1,0:T(8,128)(2,1)S(1)}, u32[]{:S(2)}, u32[]{:S(2)}) collective-permute-start(bf16[4,8,16,256]{3,2,1,0:T(8,128)(2,1)S(1)} %join.11), channel_id=1, source_target_pairs={{0,4},{1,5},{2,6},{3,7},{4,0},{5,1},{6,2},{7,3},{8,12},{9,13},{10,... | collective-permute-start | bytes 786440 | tf_op jit(solution)/shard_map/ppermute | solution.py:301
  53.7 1.6 %collective-permute-start.10 = (bf16[1,24,16,256]{3,2,1,0:T(8,128)(2,1)S(1)}, bf16[1,24,16,256]{3,2,1,0:T(8,128)(2,1)S(1)}, u32[]{:S(2)}, u32[]{:S(2)}) collective-permute-start(bf16[1,24,16,256]{3,2,1,0:T(8,128)(2,1)S(1)} %slice.33), channel_id=1, source_target_pairs={{8,0},{24,8},{16,24},{0,16},{9,1},{25,9},{17,25},{1,17},{10,2},{26... | collective-permute-start | bytes 589832 | tf_op jit(solution)/shard_map/ppermute | solution.py:257
  55.3 0.5 collective-permute-done.15.refs_3_
  55.8 1.9 %collective-permute-start.9 = (bf16[1,24,16,256]{3,2,1,0:T(8,128)(2,1)S(1)}, bf16[1,24,16,256]{3,2,1,0:T(8,128)(2,1)S(1)}, u32[]{:S(2)}, u32[]{:S(2)}) collective-permute-start(bf16[1,24,16,256]{3,2,1,0:T(8,128)(2,1)S(1)} %slice.32), channel_id=1, source_target_pairs={{0,8},{8,24},{24,16},{16,0},{1,9},{9,25},{25,17},{17,1},{2,10},{10... | collective-permute-start | bytes 589832 | tf_op jit(solution)/shard_map/ppermute | solution.py:256
  57.7 1.2 %collective-permute-done.16.refs_5_ = bf16[6,8,16,256]{3,2,1,0:T(8,128)(2,1)S(1)} collective-permute-done((bf16[6,8,16,256]{3,2,1,0:T(8,128)(2,1)S(1)}, bf16[6,8,16,256]{3,2,1,0:T(8,128)(2,1)S(1)}, u32[]{:S(2)}, u32[]{:S(2)}) %collective-permute-start.16) | collective-permute-done | bytes 393248 | tf_op jit(solution)/shard_map/ppermute | solution.py:250
  59.0 1.5 %collective-permute-start.17 = (bf16[3,8,16,256]{3,2,1,0:T(8,128)(2,1)S(1)}, bf16[3,8,16,256]{3,2,1,0:T(8,128)(2,1)S(1)}, u32[]{:S(2)}, u32[]{:S(2)}) collective-permute-start(bf16[3,8,16,256]{3,2,1,0:T(8,128)(2,1)S(1)} %slice.34), channel_id=1, source_target_pairs={{0,8},{8,24},{24,16},{16,0},{1,9},{9,25},{25,17},{17,1},{2,10},{10... | collective-permute-start | bytes 589832 | tf_op jit(solution)/shard_map/ppermute | solution.py:256
  60.4 1.5 %collective-permute-done.11.refs_1_ = bf16[4,8,16,256]{3,2,1,0:T(8,128)(2,1)S(1)} collective-permute-done((bf16[4,8,16,256]{3,2,1,0:T(8,128)(2,1)S(1)}, bf16[4,8,16,256]{3,2,1,0:T(8,128)(2,1)S(1)}, u32[]{:S(2)}, u32[]{:S(2)}) %collective-permute-start.11) | collective-permute-done | bytes 262176 | tf_op jit(solution)/shard_map/ppermute | solution.py:301
  61.9 1.5 %collective-permute-start.18 = (bf16[3,8,16,256]{3,2,1,0:T(8,128)(2,1)S(1)}, bf16[3,8,16,256]{3,2,1,0:T(8,128)(2,1)S(1)}, u32[]{:S(2)}, u32[]{:S(2)}) collective-permute-start(bf16[3,8,16,256]{3,2,1,0:T(8,128)(2,1)S(1)} %slice.35), channel_id=1, source_target_pairs={{8,0},{24,8},{16,24},{0,16},{9,1},{25,9},{17,25},{1,17},{10,2},{26... | collective-permute-start | bytes 589832 | tf_op jit(solution)/shard_map/ppermute | solution.py:257
  63.5 0.0 collective-permute-done.10.refs_7_
  63.5 0.6 collective-permute-start.12
  64.0 0.9 collective-permute-done.3.refs_2_.refs_0_
  64.9 1.5 %collective-permute-start.13 = (bf16[6,8,16,256]{3,2,1,0:T(8,128)(2,1)S(1)}, bf16[6,8,16,256]{3,2,1,0:T(8,128)(2,1)S(1)}, u32[]{:S(2)}, u32[]{:S(2)}) collective-permute-start(bf16[6,8,16,256]{3,2,1,0:T(8,128)(2,1)S(1)} %join.17.refs_1_), channel_id=1, source_target_pairs={{8,0},{24,8},{16,24},{0,16},{9,1},{25,9},{17,25},{1,17},{10,2},{26... | collective-permute-start | bytes 1179656 | tf_op jit(solution)/shard_map/ppermute | solution.py:250
  66.5 0.0 collective-permute-done.9.refs_6_
  66.5 0.1 collective-permute-start.4
  66.6 0.8 turn.5.left_ref
  67.4 0.0 collective-permute-done.17.refs_8_
  67.4 2.2 %collective-permute-done.18.refs_9_ = bf16[3,8,16,256]{3,2,1,0:T(8,128)(2,1)S(1)} collective-permute-done((bf16[3,8,16,256]{3,2,1,0:T(8,128)(2,1)S(1)}, bf16[3,8,16,256]{3,2,1,0:T(8,128)(2,1)S(1)}, u32[]{:S(2)}, u32[]{:S(2)}) %collective-permute-start.18) | collective-permute-done | bytes 196640 | tf_op jit(solution)/shard_map/ppermute | solution.py:257
  69.6 7.9 %stack.3.refs_10_ = bf16[48,2,256,1024]{3,2,1,0:T(8,128)(2,1)} custom-call(bf16[8,2,256,128]{3,2,1,0:T(8,128)(2,1)S(1)} %turn.5.left_ref, bf16[2,24,16,256]{3,2,1,0:T(8,128)(2,1)S(1)} %join.10.refs_0_, bf16[6,8,16,256]{3,2,1,0:T(8,128)(2,1)S(1)} %join.19.refs_1_, bf16[2,24,16,256]{3,2,1,0:T(8,128)(2,1)S(1)} %collective-permute-done.5.refs_2_, ...), custom_call_target="tpu_custom_call" | custom-call | flops 2147483648 | bytes 16777216 | tf_op jit(solution)/shard_map/stack/pallas_call | solution.py:221
  77.5 0.0 collective-permute-done.12.refs_3_
  77.6 0.0 collective-permute-done.13.refs_5_
  77.6 1.5 %collective-permute-start.19 = (bf16[3,8,16,256]{3,2,1,0:T(8,128)(2,1)S(1)}, bf16[3,8,16,256]{3,2,1,0:T(8,128)(2,1)S(1)}, u32[]{:S(2)}, u32[]{:S(2)}) collective-permute-start(bf16[3,8,16,256]{3,2,1,0:T(8,128)(2,1)S(1)} %slice.28), channel_id=1, source_target_pairs={{0,8},{8,24},{24,16},{16,0},{1,9},{9,25},{25,17},{17,1},{2,10},{10... | collective-permute-start | bytes 589832 | tf_op jit(solution)/shard_map/ppermute | solution.py:256
  79.1 0.6 collective-permute-start.20
  79.7 0.0 collective-permute-done.4.refs_1_
  79.8 1.5 %collective-permute-start.6 = (bf16[6,8,16,256]{3,2,1,0:T(8,128)(2,1)S(1)}, bf16[6,8,16,256]{3,2,1,0:T(8,128)(2,1)S(1)}, u32[]{:S(2)}, u32[]{:S(2)}) collective-permute-start(bf16[6,8,16,256]{3,2,1,0:T(8,128)(2,1)S(1)} %join.15.refs_1_), channel_id=1, source_target_pairs={{0,8},{8,24},{24,16},{16,0},{1,9},{9,25},{25,17},{17,1},{2,10},{10... | collective-permute-start | bytes 1179656 | tf_op jit(solution)/shard_map/ppermute | solution.py:249
  81.3 0.5 collective-permute-start.8
  81.8 0.8 turn.4.left_ref
  82.7 1.7 %collective-permute-done.19.refs_8_ = bf16[3,8,16,256]{3,2,1,0:T(8,128)(2,1)S(1)} collective-permute-done((bf16[3,8,16,256]{3,2,1,0:T(8,128)(2,1)S(1)}, bf16[3,8,16,256]{3,2,1,0:T(8,128)(2,1)S(1)}, u32[]{:S(2)}, u32[]{:S(2)}) %collective-permute-start.19) | collective-permute-done | bytes 196640 | tf_op jit(solution)/shard_map/ppermute | solution.py:256
  84.4 0.4 collective-permute-done.20.refs_9_
  84.8 7.9 %stack.4.refs_10_ = bf16[48,2,256,1024]{3,2,1,0:T(8,128)(2,1)} custom-call(bf16[8,2,256,128]{3,2,1,0:T(8,128)(2,1)S(1)} %turn.4.left_ref, bf16[2,24,16,256]{3,2,1,0:T(8,128)(2,1)S(1)} %join.10.refs_0_, bf16[6,8,16,256]{3,2,1,0:T(8,128)(2,1)S(1)} %join.17.refs_1_, ...), custom_call_target="tpu_custom_call", output_to_operand_aliasing={{}: (11, {})} | custom-call | flops 2147483648 | bytes 16777216 | tf_op jit(solution)/shard_map/stack/pallas_call | solution.py:221
  92.7 0.0 collective-permute-done.6.refs_3_
  92.8 0.0 collective-permute-done.8.refs_5_
  92.8 1.4 %collective-permute-start.21 = (bf16[3,8,16,256]{3,2,1,0:T(8,128)(2,1)S(1)}, bf16[3,8,16,256]{3,2,1,0:T(8,128)(2,1)S(1)}, u32[]{:S(2)}, u32[]{:S(2)}) collective-permute-start(bf16[3,8,16,256]{3,2,1,0:T(8,128)(2,1)S(1)} %slice.30), channel_id=1, source_target_pairs={{0,8},{8,24},{24,16},{16,0},{1,9},{9,25},{25,17},{17,1},{2,10},{10... | collective-permute-start | bytes 589832 | tf_op jit(solution)/shard_map/ppermute | solution.py:256
  94.2 0.7 collective-permute-start.22
  94.9 0.8 turn.3.left_ref
  95.8 2.7 %collective-permute-done.21.refs_8_ = bf16[3,8,16,256]{3,2,1,0:T(8,128)(2,1)S(1)} collective-permute-done((bf16[3,8,16,256]{3,2,1,0:T(8,128)(2,1)S(1)}, bf16[3,8,16,256]{3,2,1,0:T(8,128)(2,1)S(1)}, u32[]{:S(2)}, u32[]{:S(2)}) %collective-permute-start.21) | collective-permute-done | bytes 196640 | tf_op jit(solution)/shard_map/ppermute | solution.py:256
  98.5 1.4 %collective-permute-done.22.refs_9_ = bf16[3,8,16,256]{3,2,1,0:T(8,128)(2,1)S(1)} collective-permute-done((bf16[3,8,16,256]{3,2,1,0:T(8,128)(2,1)S(1)}, bf16[3,8,16,256]{3,2,1,0:T(8,128)(2,1)S(1)}, u32[]{:S(2)}, u32[]{:S(2)}) %collective-permute-start.22) | collective-permute-done | bytes 196640 | tf_op jit(solution)/shard_map/ppermute | solution.py:257
  99.9 7.9 %stack.5 = bf16[48,2,256,1024]{3,2,1,0:T(8,128)(2,1)} custom-call(bf16[8,2,256,128]{3,2,1,0:T(8,128)(2,1)S(1)} %turn.3.left_ref, bf16[2,24,16,256]{3,2,1,0:T(8,128)(2,1)S(1)} %join.10.refs_0_, bf16[6,8,16,256]{3,2,1,0:T(8,128)(2,1)S(1)} %join.15.refs_1_, ...), custom_call_target="tpu_custom_call", output_to_operand_aliasing={{}: (11, {})} | custom-call | flops 2147483648 | bytes 16777216 | tf_op jit(solution)/shard_map/stack/pallas_call | solution.py:221
  (18 shorter events, 0.3 us)
Async XLA Ops:
  0.0 2.9 %copy-start = (bf16[4,3200,256]{2,1,0:T(8,128)(2,1)S(1)}, bf16[4,3200,256]{2,1,0:T(8,128)(2,1)}, u32[]{:S(2)}) copy-start(bf16[4,3200,256]{2,1,0:T(8,128)(2,1)} %raw_ref.1) | copy-start | bytes 19660804
  2.9 0.7 copy-start.1
  3.5 0.7 copy-start.2
  4.2 2.3 %copy-start.3 = (bf16[768,3072]{1,0:T(8,128)(2,1)S(1)}, bf16[768,3072]{1,0:T(8,128)(2,1)}, u32[]{:S(2)}) copy-start(bf16[768,3072]{1,0:T(8,128)(2,1)} %constant.4.clone.table_ref) | copy-start | bytes 14155780
  6.5 0.9 copy-start.4
  14.2 2.4 %collective-permute-start = (bf16[4,24,16,256]{3,2,1,0:T(8,128)(2,1)S(1)}, bf16[4,24,16,256]{3,2,1,0:T(8,128)(2,1)S(1)}, u32[]{:S(2)}, u32[]{:S(2)}) collective-permute-start(bf16[4,24,16,256]{3,2,1,0:T(8,128)(2,1)S(1)} %get-tuple-element.15), channel_id=1, source_target_pairs={{0,1},{1,0},{2,3},{3,2},{4,5},{5,4},{6,7},{7,6},{8,9},{9,8},{10,11... | collective-permute-start | bytes 2359304 | tf_op jit(solution)/shard_map/ppermute | solution.py:287
  16.6 17.8 %collective-permute-start.5 = (bf16[2,24,16,256]{3,2,1,0:T(8,128)(2,1)S(1)}, bf16[2,24,16,256]{3,2,1,0:T(8,128)(2,1)S(1)}, u32[]{:S(2)}, u32[]{:S(2)}) collective-permute-start(bf16[2,24,16,256]{3,2,1,0:T(8,128)(2,1)S(1)} %join.10.refs_0_), channel_id=1, source_target_pairs={{0,8},{8,24},{24,16},{16,0},{1,9},{9,25},{25,17},{17,1},{2,10},{10... | collective-permute-start | bytes 1179656 | tf_op jit(solution)/shard_map/ppermute | solution.py:249
  19.5 14.9 %collective-permute-start.7 = (bf16[2,24,16,256]{3,2,1,0:T(8,128)(2,1)S(1)}, bf16[2,24,16,256]{3,2,1,0:T(8,128)(2,1)S(1)}, u32[]{:S(2)}, u32[]{:S(2)}) collective-permute-start(bf16[2,24,16,256]{3,2,1,0:T(8,128)(2,1)S(1)} %join.10.refs_0_), channel_id=1, source_target_pairs={{8,0},{24,8},{16,24},{0,16},{9,1},{25,9},{17,25},{1,17},{10,2},{26... | collective-permute-start | bytes 1179656 | tf_op jit(solution)/shard_map/ppermute | solution.py:250
  19.7 14.8 %collective-permute-start.1 = (bf16[4,8,16,256]{3,2,1,0:T(8,128)(2,1)S(1)}, bf16[4,8,16,256]{3,2,1,0:T(8,128)(2,1)S(1)}, u32[]{:S(2)}, u32[]{:S(2)}) collective-permute-start(bf16[4,8,16,256]{3,2,1,0:T(8,128)(2,1)S(1)} %join.13), channel_id=1, source_target_pairs={{0,4},{1,5},{2,6},{3,7},{4,0},{5,1},{6,2},{7,3},{8,12},{9,13},{10,... | collective-permute-start | bytes 786440 | tf_op jit(solution)/shard_map/ppermute | solution.py:301
  34.5 12.6 %collective-permute-start.14 = (bf16[4,8,16,256]{3,2,1,0:T(8,128)(2,1)S(1)}, bf16[4,8,16,256]{3,2,1,0:T(8,128)(2,1)S(1)}, u32[]{:S(2)}, u32[]{:S(2)}) collective-permute-start(bf16[4,8,16,256]{3,2,1,0:T(8,128)(2,1)S(1)} %join.18), channel_id=1, source_target_pairs={{0,2},{1,3},{2,0},{3,1},{4,6},{5,7},{6,4},{7,5},{8,10},{9,11},{10,... | collective-permute-start | bytes 786440 | tf_op jit(solution)/shard_map/ppermute | solution.py:301
  35.3 15.3 %collective-permute-start.2 = (bf16[4,8,16,256]{3,2,1,0:T(8,128)(2,1)S(1)}, bf16[4,8,16,256]{3,2,1,0:T(8,128)(2,1)S(1)}, u32[]{:S(2)}, u32[]{:S(2)}) collective-permute-start(bf16[4,8,16,256]{3,2,1,0:T(8,128)(2,1)S(1)} %join.12), channel_id=1, source_target_pairs={{0,4},{1,5},{2,6},{3,7},{4,0},{5,1},{6,2},{7,3},{8,12},{9,13},{10,... | collective-permute-start | bytes 786440 | tf_op jit(solution)/shard_map/ppermute | solution.py:301
  47.1 8.8 %collective-permute-start.15 = (bf16[6,8,16,256]{3,2,1,0:T(8,128)(2,1)S(1)}, bf16[6,8,16,256]{3,2,1,0:T(8,128)(2,1)S(1)}, u32[]{:S(2)}, u32[]{:S(2)}) collective-permute-start(bf16[6,8,16,256]{3,2,1,0:T(8,128)(2,1)S(1)} %join.19.refs_1_), channel_id=1, source_target_pairs={{0,8},{8,24},{24,16},{16,0},{1,9},{9,25},{25,17},{17,1},{2,10},{10... | collective-permute-start | bytes 1179656 | tf_op jit(solution)/shard_map/ppermute | solution.py:249
  48.6 10.3 %collective-permute-start.16 = (bf16[6,8,16,256]{3,2,1,0:T(8,128)(2,1)S(1)}, bf16[6,8,16,256]{3,2,1,0:T(8,128)(2,1)S(1)}, u32[]{:S(2)}, u32[]{:S(2)}) collective-permute-start(bf16[6,8,16,256]{3,2,1,0:T(8,128)(2,1)S(1)} %join.19.refs_1_), channel_id=1, source_target_pairs={{8,0},{24,8},{16,24},{0,16},{9,1},{25,9},{17,25},{1,17},{10,2},{26... | collective-permute-start | bytes 1179656 | tf_op jit(solution)/shard_map/ppermute | solution.py:250
  50.6 11.3 %collective-permute-start.11 = (bf16[4,8,16,256]{3,2,1,0:T(8,128)(2,1)S(1)}, bf16[4,8,16,256]{3,2,1,0:T(8,128)(2,1)S(1)}, u32[]{:S(2)}, u32[]{:S(2)}) collective-permute-start(bf16[4,8,16,256]{3,2,1,0:T(8,128)(2,1)S(1)} %join.16), channel_id=1, source_target_pairs={{0,2},{1,3},{2,0},{3,1},{4,6},{5,7},{6,4},{7,5},{8,10},{9,11},{10,... | collective-permute-start | bytes 786440 | tf_op jit(solution)/shard_map/ppermute | solution.py:301
  50.9 14.0 %collective-permute-start.3 = (bf16[4,8,16,256]{3,2,1,0:T(8,128)(2,1)S(1)}, bf16[4,8,16,256]{3,2,1,0:T(8,128)(2,1)S(1)}, u32[]{:S(2)}, u32[]{:S(2)}) collective-permute-start(bf16[4,8,16,256]{3,2,1,0:T(8,128)(2,1)S(1)} %join.11), channel_id=1, source_target_pairs={{0,4},{1,5},{2,6},{3,7},{4,0},{5,1},{6,2},{7,3},{8,12},{9,13},{10,... | collective-permute-start | bytes 786440 | tf_op jit(solution)/shard_map/ppermute | solution.py:301
  53.7 9.8 %collective-permute-start.10 = (bf16[1,24,16,256]{3,2,1,0:T(8,128)(2,1)S(1)}, bf16[1,24,16,256]{3,2,1,0:T(8,128)(2,1)S(1)}, u32[]{:S(2)}, u32[]{:S(2)}) collective-permute-start(bf16[1,24,16,256]{3,2,1,0:T(8,128)(2,1)S(1)} %slice.33), channel_id=1, source_target_pairs={{8,0},{24,8},{16,24},{0,16},{9,1},{25,9},{17,25},{1,17},{10,2},{26... | collective-permute-start | bytes 589832 | tf_op jit(solution)/shard_map/ppermute | solution.py:257
  55.8 10.6 %collective-permute-start.9 = (bf16[1,24,16,256]{3,2,1,0:T(8,128)(2,1)S(1)}, bf16[1,24,16,256]{3,2,1,0:T(8,128)(2,1)S(1)}, u32[]{:S(2)}, u32[]{:S(2)}) collective-permute-start(bf16[1,24,16,256]{3,2,1,0:T(8,128)(2,1)S(1)} %slice.32), channel_id=1, source_target_pairs={{0,8},{8,24},{24,16},{16,0},{1,9},{9,25},{25,17},{17,1},{2,10},{10... | collective-permute-start | bytes 589832 | tf_op jit(solution)/shard_map/ppermute | solution.py:256
  59.0 8.5 %collective-permute-start.17 = (bf16[3,8,16,256]{3,2,1,0:T(8,128)(2,1)S(1)}, bf16[3,8,16,256]{3,2,1,0:T(8,128)(2,1)S(1)}, u32[]{:S(2)}, u32[]{:S(2)}) collective-permute-start(bf16[3,8,16,256]{3,2,1,0:T(8,128)(2,1)S(1)} %slice.34), channel_id=1, source_target_pairs={{0,8},{8,24},{24,16},{16,0},{1,9},{9,25},{25,17},{17,1},{2,10},{10... | collective-permute-start | bytes 589832 | tf_op jit(solution)/shard_map/ppermute | solution.py:256
  61.9 7.7 %collective-permute-start.18 = (bf16[3,8,16,256]{3,2,1,0:T(8,128)(2,1)S(1)}, bf16[3,8,16,256]{3,2,1,0:T(8,128)(2,1)S(1)}, u32[]{:S(2)}, u32[]{:S(2)}) collective-permute-start(bf16[3,8,16,256]{3,2,1,0:T(8,128)(2,1)S(1)} %slice.35), channel_id=1, source_target_pairs={{8,0},{24,8},{16,24},{0,16},{9,1},{25,9},{17,25},{1,17},{10,2},{26... | collective-permute-start | bytes 589832 | tf_op jit(solution)/shard_map/ppermute | solution.py:257
  63.5 14.1 %collective-permute-start.12 = (bf16[6,8,16,256]{3,2,1,0:T(8,128)(2,1)S(1)}, bf16[6,8,16,256]{3,2,1,0:T(8,128)(2,1)S(1)}, u32[]{:S(2)}, u32[]{:S(2)}) collective-permute-start(bf16[6,8,16,256]{3,2,1,0:T(8,128)(2,1)S(1)} %join.17.refs_1_), channel_id=1, source_target_pairs={{0,8},{8,24},{24,16},{16,0},{1,9},{9,25},{25,17},{17,1},{2,10},{10... | collective-permute-start | bytes 1179656 | tf_op jit(solution)/shard_map/ppermute | solution.py:249
  64.9 12.6 %collective-permute-start.13 = (bf16[6,8,16,256]{3,2,1,0:T(8,128)(2,1)S(1)}, bf16[6,8,16,256]{3,2,1,0:T(8,128)(2,1)S(1)}, u32[]{:S(2)}, u32[]{:S(2)}) collective-permute-start(bf16[6,8,16,256]{3,2,1,0:T(8,128)(2,1)S(1)} %join.17.refs_1_), channel_id=1, source_target_pairs={{8,0},{24,8},{16,24},{0,16},{9,1},{25,9},{17,25},{1,17},{10,2},{26... | collective-permute-start | bytes 1179656 | tf_op jit(solution)/shard_map/ppermute | solution.py:250
  66.5 13.2 %collective-permute-start.4 = (bf16[4,8,16,256]{3,2,1,0:T(8,128)(2,1)S(1)}, bf16[4,8,16,256]{3,2,1,0:T(8,128)(2,1)S(1)}, u32[]{:S(2)}, u32[]{:S(2)}) collective-permute-start(bf16[4,8,16,256]{3,2,1,0:T(8,128)(2,1)S(1)} %join.14), channel_id=1, source_target_pairs={{0,2},{1,3},{2,0},{3,1},{4,6},{5,7},{6,4},{7,5},{8,10},{9,11},{10,... | collective-permute-start | bytes 786440 | tf_op jit(solution)/shard_map/ppermute | solution.py:301
  77.6 6.8 %collective-permute-start.19 = (bf16[3,8,16,256]{3,2,1,0:T(8,128)(2,1)S(1)}, bf16[3,8,16,256]{3,2,1,0:T(8,128)(2,1)S(1)}, u32[]{:S(2)}, u32[]{:S(2)}) collective-permute-start(bf16[3,8,16,256]{3,2,1,0:T(8,128)(2,1)S(1)} %slice.28), channel_id=1, source_target_pairs={{0,8},{8,24},{24,16},{16,0},{1,9},{9,25},{25,17},{17,1},{2,10},{10... | collective-permute-start | bytes 589832 | tf_op jit(solution)/shard_map/ppermute | solution.py:256
  79.1 5.7 %collective-permute-start.20 = (bf16[3,8,16,256]{3,2,1,0:T(8,128)(2,1)S(1)}, bf16[3,8,16,256]{3,2,1,0:T(8,128)(2,1)S(1)}, u32[]{:S(2)}, u32[]{:S(2)}) collective-permute-start(bf16[3,8,16,256]{3,2,1,0:T(8,128)(2,1)S(1)} %slice.29), channel_id=1, source_target_pairs={{8,0},{24,8},{16,24},{0,16},{9,1},{25,9},{17,25},{1,17},{10,2},{26... | collective-permute-start | bytes 589832 | tf_op jit(solution)/shard_map/ppermute | solution.py:257
  79.8 13.0 %collective-permute-start.6 = (bf16[6,8,16,256]{3,2,1,0:T(8,128)(2,1)S(1)}, bf16[6,8,16,256]{3,2,1,0:T(8,128)(2,1)S(1)}, u32[]{:S(2)}, u32[]{:S(2)}) collective-permute-start(bf16[6,8,16,256]{3,2,1,0:T(8,128)(2,1)S(1)} %join.15.refs_1_), channel_id=1, source_target_pairs={{0,8},{8,24},{24,16},{16,0},{1,9},{9,25},{25,17},{17,1},{2,10},{10... | collective-permute-start | bytes 1179656 | tf_op jit(solution)/shard_map/ppermute | solution.py:249
  81.3 11.5 %collective-permute-start.8 = (bf16[6,8,16,256]{3,2,1,0:T(8,128)(2,1)S(1)}, bf16[6,8,16,256]{3,2,1,0:T(8,128)(2,1)S(1)}, u32[]{:S(2)}, u32[]{:S(2)}) collective-permute-start(bf16[6,8,16,256]{3,2,1,0:T(8,128)(2,1)S(1)} %join.15.refs_1_), channel_id=1, source_target_pairs={{8,0},{24,8},{16,24},{0,16},{9,1},{25,9},{17,25},{1,17},{10,2},{26... | collective-permute-start | bytes 1179656 | tf_op jit(solution)/shard_map/ppermute | solution.py:250
  92.8 5.7 %collective-permute-start.21 = (bf16[3,8,16,256]{3,2,1,0:T(8,128)(2,1)S(1)}, bf16[3,8,16,256]{3,2,1,0:T(8,128)(2,1)S(1)}, u32[]{:S(2)}, u32[]{:S(2)}) collective-permute-start(bf16[3,8,16,256]{3,2,1,0:T(8,128)(2,1)S(1)} %slice.30), channel_id=1, source_target_pairs={{0,8},{8,24},{24,16},{16,0},{1,9},{9,25},{25,17},{17,1},{2,10},{10... | collective-permute-start | bytes 589832 | tf_op jit(solution)/shard_map/ppermute | solution.py:256
  94.2 5.7 %collective-permute-start.22 = (bf16[3,8,16,256]{3,2,1,0:T(8,128)(2,1)S(1)}, bf16[3,8,16,256]{3,2,1,0:T(8,128)(2,1)S(1)}, u32[]{:S(2)}, u32[]{:S(2)}) collective-permute-start(bf16[3,8,16,256]{3,2,1,0:T(8,128)(2,1)S(1)} %slice.31), channel_id=1, source_target_pairs={{8,0},{24,8},{16,24},{0,16},{9,1},{25,9},{17,25},{1,17},{10,2},{26... | collective-permute-start | bytes 589832 | tf_op jit(solution)/shard_map/ppermute | solution.py:257
